TPU v7x, 32 devices: a whole 2x2x4 slice. The times are simulated.
32 devices in a mesh: grp: 2 (over x), mod: 16 (over z, y, core).
Axes of the slice: x: 2, y: 2, z: 4, core: 2. Of those that a mesh axis runs over, the one named last changes fastest.
Arguments:
- inputs_proj: bfloat16 [128, 16, 1536], P(('grp', 'mod')), parts along dimension 0, may hold values from -2.5 to 2.5
- outputs_proj: bfloat16 [128, 16, 1280], P(('grp', 'mod')), parts along dimension 0, may hold values from -2.5 to 2.5
- lengths: int32 [128], P(('grp', 'mod')), parts along dimension 0, may hold values from 16 to 32, as said below
- owner: int32 [16], replicated, may hold values from 0 to 15, each once
- fisher_inv: bfloat16 [16, 1920, 1920], P('mod'), may hold values from -25 to 25, as said below
- query_grads: bfloat16 [16, 512, 1920], P('mod'), may hold values from -0.03125 to 0.03125
Outputs:
- scores: float32 [128, 512], P(('grp', 'mod')), parts along dimension 0
There are 2 independent parts, one for each index of `grp`. A program takes and returns all parts, laid end to end along the dimension named above; an argument that names none is the same for every part. Nothing has to cross between parts.
Inputs may be any that keep to these rules, and one draw needn't show every extreme that they name: `fisher_inv`: each matrix is symmetric. `lengths`: some example of each group has all 32 slots live.
All inputs are finite; a program needn't handle non-finite values.
Results may differ from a plain program's by a relative error of at most 0.0041.
Values may be sent and summed in bfloat16 or wider, within the bound.
A program may use at most 128 MiB of HBM per device.

v0:
```python
import jax
import jax.numpy as jnp
from jax import lax
from jax.sharding import PartitionSpec as P

OUT_RANK = 40
IN_RANK = 48
SEQ_LEN = 32


def masked(source, lengths, features):
    count_rows = source.shape[0]
    count_modules = source.shape[1]
    live = (lax.broadcasted_iota(jnp.int32, (count_rows, SEQ_LEN), 1) < lengths[:, None]).astype(
        source.dtype
    )
    return source.reshape(count_rows, count_modules, features, SEQ_LEN) * live[:, None, None, :]


def outer_grads(side_out, side_in):
    formed = jnp.einsum("emol,emil->emoi", side_out, side_in, preferred_element_type=jnp.float32)
    return formed.astype(jnp.bfloat16)


def local(inputs_proj, outputs_proj, lengths, owner, fisher_inv, query_grads):
    count_modules = owner.shape[0]
    local_rows = inputs_proj.shape[0]
    local_in = masked(inputs_proj, lengths, IN_RANK)
    local_out = masked(outputs_proj, lengths, OUT_RANK)
    inverse = (
        jnp.zeros((count_modules,), jnp.int32)
        .at[owner]
        .set(jnp.arange(count_modules, dtype=jnp.int32))
    )
    precond = jnp.dot(query_grads[0], fisher_inv[0], preferred_element_type=jnp.float32).astype(
        jnp.bfloat16
    )
    formed = outer_grads(local_out, local_in).reshape(local_rows, count_modules, OUT_RANK * IN_RANK)
    routed = jnp.take(formed, inverse, axis=1)
    received = lax.all_to_all(routed, "mod", split_axis=1, concat_axis=0, tiled=True)
    example_grads = received.reshape(received.shape[0], OUT_RANK * IN_RANK)
    return lax.psum_scatter(
        lax.dot_general(
            example_grads, precond, (((1,), (1,)), ((), ())), preferred_element_type=jnp.float32
        ),
        "mod",
        scatter_dimension=0,
        tiled=True,
    )


def solution(mesh):
    return jax.shard_map(
        local,
        mesh=mesh,
        in_specs=(
            P(("grp", "mod"), None, None),
            P(("grp", "mod"), None, None),
            P(("grp", "mod")),
            P(),
            P("mod", None, None),
            P("mod", None, None),
        ),
        out_specs=P(("grp", "mod"), None),
        check_vma=False,
    )
```

profile of v0, /device:TPU:0, one launch (start us, length us, event | category | flops | bytes accessed | tf_op | source)
XLA Modules:
  0.0 134.9 jit_solution(4244372473379199005)
XLA Ops:
  6.5 0.0 copy-start
  6.5 0.0 all-reduce.3.cloned.1.call-start
  6.5 0.8 compare_select_fusion.1
  7.3 0.6 scatter_custom_fusion
  8.0 1.5 %reshape.35 = bf16[4,16,48,32]{3,2,1,0:T(8,128)(2,1)S(1)} reshape(bf16[4,16,1536]{2,1,0:T(8,128)(2,1)} %param.6) | data formatting | bytes 393216 | tf_op jit(solution)/shard_map/reshape | solution.py:17
  9.5 2.3 %reshape.34 = bf16[4,16,40,32]{3,2,1,0:T(8,128)(2,1)} reshape(bf16[4,16,1280]{2,1,0:T(8,128)(2,1)} %param.7) | data formatting | bytes 327680 | tf_op jit(solution)/shard_map/reshape | solution.py:17
  11.7 0.7 fusion.15
  12.4 1.6 %convolution_convert_fusion = bf16[4,16,40,48]{3,2,1,0:T(8,128)(2,1)S(1)} fusion(bf16[4,16,48,32]{3,2,1,0:T(8,128)(2,1)S(1)} %reshape.35, bf16[4,16,40,32]{3,2,1,0:T(8,128)(2,1)} %reshape.34, bf16[4,32]{1,0:T(4,128)(2,1)S(1)} %fusion.15), kind=kOutput, calls=%fused_computation.6 | convolution fusion | flops 8167424 | bytes 606464 | tf_op jit(solution)/shard_map/emol,emil->emoi/dot_general | solution.py:21
  14.1 0.4 reshape.36
  14.5 0.1 copy.14
  14.6 0.8 gather_fusion
  15.4 0.2 select_bitcast_fusion
  15.6 17.0 %all_to_all.15 = bf16[4,16,1920]{2,0,1:T(4,128)(2,1)S(1)} all-to-all(bf16[4,16,1920]{2,0,1:T(4,128)(2,1)S(1)} %select_bitcast_fusion), channel_id=1, replica_groups=mesh['grp'=2,'mod'=16] {'mod'}, dimensions={1} | all-to-all | bytes 491520 | tf_op jit(solution)/shard_map/all_to_all | solution.py:40
  32.6 0.1 reshape.37
  32.6 0.0 copy-done
  32.6 0.0 copy-start.1
  32.7 8.7 %fusion.8 = f32[64,512]{1,0:T(8,128)} fusion(bf16[64,1920]{1,0:T(8,128)(2,1)S(1)} %reshape.37, bf16[1,1920,1920]{2,1,0:T(8,128)(2,1)} %param.10, bf16[1,512,1920]{2,1,0:T(8,128)(2,1)S(1)} %copy-done), kind=kOutput, calls=%fused_computation.7 | convolution fusion | flops 3901685760 | bytes 9715712 | tf_op jit(solution)/shard_map/dot_general | solution.py:43
  41.4 0.0 all-reduce.3.cloned.1.call-update
  41.4 0.0 copy-done.1
  41.4 0.6 dynamic-slice
  42.7 84.0 %all-reduce.3.cloned.1.call-done = f32[64,512]{1,0:T(8,128)} async-done(((f32[64,512]{1,0:T(8,128)}), f32[64,512]{1,0:T(8,128)}) %all-reduce.3.cloned.1.call-update) | async-done | bytes 131088
  126.7 1.3 constant_dynamic-slice_fusion
  (4 shorter events, 0.0 us)
Async XLA Ops:
  6.5 26.1 %copy-start = (bf16[1,512,1920]{2,1,0:T(8,128)(2,1)S(1)}, bf16[1,512,1920]{2,1,0:T(8,128)(2,1)}, u32[]{:S(2)}) copy-start(bf16[1,512,1920]{2,1,0:T(8,128)(2,1)} %param.11) | copy-start | bytes 5898244
  6.5 120.2 %all-reduce.3.cloned.1.call-start = ((), (), s32[]{:S(2)}) async-start(), calls=%async_computation.1 | async-start | bytes 262144
  32.6 8.8 %copy-start.1 = (u32[32]{0:T(128)S(1)}, u32[32]{0:T(128)}, u32[]{:S(2)}) copy-start(u32[32]{0:T(128)} %constant.25) | copy-start | bytes 388
Sparse Core Ops, SparseCore 0:
  41.5 85.1 all-reduce.2
where the time goes:
time: 136 us; the launch traced here: 135 us
  waiting for transfers between devices  84.1 us (62%)
  blocking collectives  17 us (12%)
  between operations  14.1 us (10%)
  matrix products  10.4 us (8%)
  local copies, waits for them, and re-layouts  7.6 us (6%)
  other arithmetic  1.73 us (1%)
    unnamed x2, waiting for transfers between devices  84.1 us
    all_to_all x1, blocking collectives, local(): lax.all_to_all(routed, 'mod', split_axis=1, concat_axis=0, tiled=True)  17 us
    dot_general x1, matrix products, local(): lax.dot_general(example_grads, precond, (((1,), (1,)), ((), ())), preferr...  8.73 us
    reshape x2, local copies, waits for them, and re-layouts, masked(): source.reshape(count_rows, count_modules, features, SEQ_LEN)  3.71 us
  transfers between devices with their start and end apart: 1, of which 1 were waited for; matrix products, arithmetic and copies ran while one was open for 0% of the time, Pallas kernels for 0%

commit v1 on v0

v1 whole, which is shorter than its diff:
```python
import functools
import math

import jax
import jax.numpy as jnp
from jax import lax
from jax.experimental import pallas as pl
from jax.experimental.pallas import tpu as pltpu
from jax.sharding import PartitionSpec as P

MESH = pl.DeviceIdType.MESH
F32 = jnp.float32
BF16 = jnp.bfloat16
NT = (((1,), (1,)), ((), ()))

LANES = 128
WIDE = 256
PACK = 16
SUB = 8


def nt(a, b):
    return lax.dot_general(a, b, NT, preferred_element_type=F32)


def kernel(
    n,
    owner_ref,
    len_ref,
    in_ref,
    out_ref,
    f_hbm,
    q_hbm,
    res_ref,
    f_v,
    q_v,
    it_ref,
    ot_ref,
    gt_ref,
    p_ref,
    send_ref,
    recv_ref,
    rs_send,
    rs_recv,
    f_sem,
    q_sem,
    g_send_sem,
    g_recv_sem,
    s_send_sem,
    s_recv_sem,
):
    me = lax.axis_index("mod")
    rows = in_ref.shape[0]
    grad = f_hbm.shape[1]
    queries = q_hbm.shape[1]
    seq = math.isqrt(in_ref.shape[2] * out_ref.shape[2] // grad)
    rank_in = in_ref.shape[2] // seq
    rank_out = out_ref.shape[2] // seq
    quarters = PACK // rows
    outer = rank_out // quarters
    depth = outer * rank_in
    dests = WIDE // PACK
    groups = n // dests
    chunks_in = in_ref.shape[2] // WIDE
    chunks_out = out_ref.shape[2] // WIDE
    in_low = WIDE // seq
    out_low = WIDE // (seq * quarters)
    f_blocks = f_sem.shape[0]
    f_rows = grad // f_blocks

    def f_copy(b):
        where = pl.ds(b * f_rows, f_rows)
        return pltpu.make_async_copy(f_hbm.at[0, where], f_v.at[where], f_sem.at[b])

    q_copy = pltpu.make_async_copy(q_hbm.at[0], q_v, q_sem)
    q_copy.start()
    for b in range(f_blocks):
        f_copy(b).start()

    barrier = pltpu.get_barrier_semaphore()

    @pl.loop(1, n)
    def _(k):
        pl.semaphore_signal(
            barrier, inc=1, device_id={"mod": lax.rem(me + k, n)}, device_id_type=MESH
        )

    span = rows * n
    lane = lax.broadcasted_iota(jnp.int32, (1, span), 1)
    held = lax.fori_loop(
        0,
        n,
        lambda m, v: jnp.where(lax.rem(lane, n) == m, owner_ref[m], v),
        jnp.zeros((1, span), jnp.int32),
    )

    a = lax.broadcasted_iota(jnp.int32, (WIDE, WIDE), 0)
    b = lax.broadcasted_iota(jnp.int32, (WIDE, WIDE), 1)
    swap = ((a // in_low == b % seq) & (a % in_low == b // seq)).astype(BF16)
    eye = (a == b).astype(BF16)
    a = lax.broadcasted_iota(jnp.int32, (out_low * seq, WIDE), 0)
    b = lax.broadcasted_iota(jnp.int32, (out_low * seq, WIDE), 1)
    fold = ((a // seq == b // (seq * quarters)) & (a % seq == b % seq)).astype(BF16)

    a = lax.broadcasted_iota(jnp.int32, (WIDE, WIDE), 0)
    limit = jnp.zeros((WIDE, WIDE), jnp.int32)
    for e in range(rows):
        limit = jnp.where(a % rows == e, len_ref[e], limit)
    live = ((b_lane := lax.broadcasted_iota(jnp.int32, (WIDE, WIDE), 1)) % seq < limit) & (
        (b_lane // seq) % quarters == (a % PACK) // rows
    )

    gt_ref[pl.ds(depth, gt_ref.shape[0] - depth), :] = jnp.zeros(
        (gt_ref.shape[0] - depth, WIDE), F32
    )
    for s in range(quarters):
        p_ref[s, pl.ds(depth, p_ref.shape[1] - depth), :] = jnp.zeros(
            (p_ref.shape[1] - depth, queries), BF16
        )

    @pl.loop(0, groups)
    def _(g):
        row = lax.broadcasted_iota(jnp.int32, (WIDE, span), 0)
        col = lax.broadcasted_iota(jnp.int32, (WIDE, span), 1)
        pick = ((held == g * dests + row // PACK) & (col // n == row % rows)).astype(BF16)

        for c in range(chunks_in):
            x = in_ref[:, :, c * WIDE : (c + 1) * WIDE].reshape(span, WIDE)
            y = jnp.dot(pick, x, preferred_element_type=F32).astype(BF16)
            it_ref[c] = nt(swap, y)
        for c in range(chunks_out):
            x = out_ref[:, :, c * WIDE : (c + 1) * WIDE].reshape(span, WIDE)
            y = jnp.dot(pick, x, preferred_element_type=F32)
            y = jnp.where(live, y, 0.0).astype(BF16)
            ot_ref[pl.ds(c * out_low * seq, out_low * seq), :] = nt(fold, y)

        step = outer // 2
        for half in range(WIDE // LANES):
            at = pl.ds(half * LANES, LANES)
            for first in range(0, outer, step):

                def add(t8, acc):
                    acc = list(acc)
                    base = pl.multiple_of(t8 * SUB, SUB)
                    fos = [ot_ref[pl.ds((first + o) * seq + base, SUB), at] for o in range(step)]
                    for tt in range(SUB):
                        t = t8 * SUB + tt
                        fi = [
                            it_ref[c, pl.ds(pl.multiple_of(t * in_low, in_low), in_low), at]
                            for c in range(chunks_in)
                        ]
                        for o in range(step):
                            fo = fos[o][tt : tt + 1]
                            for c in range(chunks_in):
                                acc[o * chunks_in + c] = acc[o * chunks_in + c] + fi[c] * fo
                    return tuple(acc)

                acc = lax.fori_loop(
                    0,
                    seq // SUB,
                    add,
                    tuple(jnp.zeros((in_low, LANES), F32) for _ in range(step * chunks_in)),
                )
                for o in range(step):
                    for c in range(chunks_in):
                        gt_ref[pl.ds((first + o) * rank_in + c * in_low, in_low), at] = acc[
                            o * chunks_in + c
                        ]

        formed = nt(eye, gt_ref[...].astype(BF16)).astype(BF16)
        send_ref[pl.ds(g * dests, dests)] = formed.reshape(dests, PACK, formed.shape[1])

    pl.semaphore_wait(barrier, n - 1)

    def g_copy(dst, slot):
        return pltpu.make_async_remote_copy(
            src_ref=send_ref.at[dst],
            dst_ref=recv_ref.at[slot],
            send_sem=g_send_sem.at[dst],
            recv_sem=g_recv_sem.at[slot],
            device_id={"mod": dst},
            device_id_type=MESH,
        )

    def s_copy(dst, slot):
        return pltpu.make_async_remote_copy(
            src_ref=rs_send.at[dst],
            dst_ref=rs_recv.at[slot],
            send_sem=s_send_sem.at[dst],
            recv_sem=s_recv_sem.at[slot],
            device_id={"mod": dst},
            device_id_type=MESH,
        )

    @pl.loop(1, n)
    def _(k):
        g_copy(lax.rem(me + k, n), me).start()

    recv_ref[me] = send_ref[me]

    q_copy.wait()
    for blk in range(f_blocks):
        f_copy(blk).wait()
        part = nt(f_v[blk * f_rows : (blk + 1) * f_rows, :], q_v[...]).astype(BF16)
        for o in range(f_rows // rank_in):
            whole = blk * (f_rows // rank_in) + o
            p_ref[whole % quarters, pl.ds((whole // quarters) * rank_in, rank_in), :] = part[
                o * rank_in : (o + 1) * rank_in
            ]

    @pl.loop(1, n)
    def _(k):
        src = lax.rem(me + n - k, n)
        g_copy(src, src).wait_recv()

    @pl.loop(0, groups)
    def _(g):
        got = recv_ref[pl.ds(g * dests, dests)].reshape(WIDE, p_ref.shape[1])
        row = lax.broadcasted_iota(jnp.int32, got.shape, 0)
        total = jnp.zeros((WIDE, queries), F32)
        for s in range(quarters):
            mine = ((row % PACK) // rows == s).astype(F32).astype(BF16)
            total = total + jnp.dot(got * mine, p_ref[s], preferred_element_type=F32)
        total = total.reshape(dests, PACK, queries)
        total = total[:, :SUB] + total[:, SUB:]
        total = total + pltpu.roll(total, rows, 1)
        row = lax.broadcasted_iota(jnp.int32, (dests, SUB, queries // 2), 1)
        rs_send[pl.ds(g * dests, dests)] = jnp.where(
            row < rows, total[:, :, : queries // 2], total[:, :, queries // 2 :]
        )

    @pl.loop(1, n)
    def _(k):
        s_copy(lax.rem(me + k, n), me).start()

    rs_recv[me] = rs_send[me]

    @pl.loop(1, n)
    def _(k):
        src = lax.rem(me + n - k, n)
        s_copy(src, src).wait_recv()

    total = rs_recv[0]
    if n <= 32:
        for src in range(1, n):
            total = total + rs_recv[src]
    else:
        total = lax.fori_loop(1, n, lambda src, v: v + rs_recv[src], total)
    res_ref[:, : queries // 2] = total[:rows]
    res_ref[:, queries // 2 :] = total[rows:]

    @pl.loop(1, n)
    def _(k):
        dst = lax.rem(me + k, n)
        g_copy(dst, me).wait_send()
        s_copy(dst, me).wait_send()


def local(n, inputs_proj, outputs_proj, lengths, owner, fisher_inv, query_grads):
    rows = inputs_proj.shape[0]
    grad = fisher_inv.shape[1]
    queries = query_grads.shape[1]
    quarters = PACK // rows
    depth = grad // quarters
    padded = -(-depth // LANES) * LANES
    f_blocks = 4
    smem = pl.BlockSpec(memory_space=pltpu.SMEM)
    vmem = pl.BlockSpec(memory_space=pltpu.VMEM)
    hbm = pl.BlockSpec(memory_space=pl.ANY)
    return pl.pallas_call(
        functools.partial(kernel, n),
        out_shape=jax.ShapeDtypeStruct((rows, queries), F32),
        in_specs=[smem, smem, vmem, vmem, hbm, hbm],
        out_specs=vmem,
        scratch_shapes=[
            pltpu.VMEM((grad, grad), BF16),
            pltpu.VMEM((queries, grad), BF16),
            pltpu.VMEM((inputs_proj.shape[2] // WIDE, WIDE, WIDE), F32),
            pltpu.VMEM((outputs_proj.shape[2] // quarters, WIDE), F32),
            pltpu.VMEM((padded, WIDE), F32),
            pltpu.VMEM((quarters, padded, queries), BF16),
            pltpu.VMEM((n, PACK, padded), BF16),
            pltpu.VMEM((n, PACK, padded), BF16),
            pltpu.VMEM((n, SUB, queries // 2), F32),
            pltpu.VMEM((n, SUB, queries // 2), F32),
            pltpu.SemaphoreType.DMA((f_blocks,)),
            pltpu.SemaphoreType.DMA,
            pltpu.SemaphoreType.DMA((n,)),
            pltpu.SemaphoreType.DMA((n,)),
            pltpu.SemaphoreType.DMA((n,)),
            pltpu.SemaphoreType.DMA((n,)),
        ],
        compiler_params=pltpu.CompilerParams(
            collective_id=0, has_side_effects=True, vmem_limit_bytes=50 * 1024 * 1024
        ),
    )(owner, lengths, inputs_proj, outputs_proj, fisher_inv, query_grads)


def solution(mesh):
    return jax.shard_map(
        functools.partial(local, mesh.shape["mod"]),
        mesh=mesh,
        in_specs=(
            P(("grp", "mod"), None, None),
            P(("grp", "mod"), None, None),
            P(("grp", "mod")),
            P(),
            P("mod", None, None),
            P("mod", None, None),
        ),
        out_specs=P(("grp", "mod"), None),
        check_vma=False,
    )
```

time: 136 us -> 26 us (0.19)
  waiting for transfers between devices: 84.1 us -> 0 us
  Pallas kernels: 0 us -> 20.4 us
  blocking collectives: 17 us -> 0 us
  between operations: 14.1 us -> 0.01 us
  matrix products: 10.4 us -> 0 us
  local copies, waits for them, and re-layouts: 7.6 us -> 5.3 us
  other arithmetic: 1.73 us -> 0 us
    unnamed x2 -> x0, waiting for transfers between devices: 84.1 us -> none
    pallas_call x0 -> x1, Pallas kernels: none -> 20.4 us  [local(): pl.pallas_call(functools.partial(kernel, n), out_shape=jax.ShapeDtypeStru...]
    all_to_all x1 -> x0, blocking collectives: 17 us -> none  [local(): lax.all_to_all(routed, 'mod', split_axis=1, concat_axis=0, tiled=True)]
    dot_general x2 -> x0, matrix products: 10.4 us -> none  [the longest x1 8.73 us: local(): lax.dot_general(example_grads, precond, (((1,), (1,)), ((), ())), preferr...]
    reshape x5 -> x0, local copies, waits for them, and re-layouts: 4.3 us -> none  [the longest x2 3.71 us: masked(): source.reshape(count_rows, count_modules, features, SEQ_LEN)]
    unnamed x6 -> x11, local copies, waits for them, and re-layouts: 1.92 us -> 5.3 us
  transfers between devices with their start and end apart: 1 -> 0, of which waited for: 1 -> 0; matrix products, arithmetic and copies ran while one was open for 0% -> 0% of each run, Pallas kernels for 0% -> 0%
where the time goes in v1:
time: 26 us; the launch traced here: 25.7 us
  Pallas kernels  20.4 us (78%)
  local copies, waits for them, and re-layouts  5.3 us (20%)
    pallas_call x1, Pallas kernels, local(): pl.pallas_call(functools.partial(kernel, n), out_shape=jax.ShapeDtypeStru...  20.4 us
    unnamed x11, local copies, waits for them, and re-layouts  5.3 us

profile of v1, /device:TPU:0, one launch (start us, length us, event | category | flops | bytes accessed | tf_op | source)
XLA Modules:
  0.0 25.7 jit_solution(17994418357416290000)
XLA Ops:
  0.0 0.0 copy-start
  0.0 1.5 %copy-done = bf16[1,512,1920]{2,1,0:T(8,128)(2,1)S(1)} copy-done((bf16[1,512,1920]{2,1,0:T(8,128)(2,1)S(1)}, bf16[1,512,1920]{2,1,0:T(8,128)(2,1)}, u32[]{:S(2)}) %copy-start) | copy-done | bytes 1966104
  1.5 0.0 copy-start.1
  1.5 0.9 %copy-done.1 = bf16[4,16,1536]{2,1,0:T(8,128)(2,1)S(1)} copy-done((bf16[4,16,1536]{2,1,0:T(8,128)(2,1)S(1)}, bf16[4,16,1536]{2,1,0:T(8,128)(2,1)}, u32[]{:S(2)}) %copy-start.1) | copy-done | bytes 196632
  2.5 0.0 copy-start.2
  2.5 0.9 %copy-done.2 = bf16[4,16,1280]{2,1,0:T(8,128)(2,1)S(1)} copy-done((bf16[4,16,1280]{2,1,0:T(8,128)(2,1)S(1)}, bf16[4,16,1280]{2,1,0:T(8,128)(2,1)}, u32[]{:S(2)}) %copy-start.2) | copy-done | bytes 163864
  3.4 0.0 copy-start.3
  3.4 0.7 %copy-done.3 = s32[16]{0:T(128)S(1)} copy-done((s32[16]{0:T(128)S(1)}, s32[16]{0:T(128)}, u32[]{:S(2)}) %copy-start.3) | copy-done | bytes 88
  4.0 0.0 copy-start.4
  4.0 0.7 %copy-done.4 = s32[4]{0:T(128)S(1)} copy-done((s32[4]{0:T(128)S(1)}, s32[4]{0:T(128)}, u32[]{:S(2)}) %copy-start.4) | copy-done | bytes 40
  4.7 20.4 %shard_map.64 = f32[4,512]{1,0:T(4,128)S(1)} custom-call(s32[16]{0:T(128)S(1)} %copy-done.3, s32[4]{0:T(128)S(1)} %copy-done.4, bf16[4,16,1536]{2,1,0:T(8,128)(2,1)S(1)} %copy-done.1, bf16[4,16,1280]{2,1,0:T(8,128)(2,1)S(1)} %copy-done.2, bf16[1,1920,1920]{2,1,0:T(8,128)(2,1)} %f_hbm.1, bf16[1,512,1920]{2,1,0:T(8,128)(2,1)S(1)} %copy-done), custom_call_target="tpu_custom_call" | custom-call | tf_op jit(solution)/shard_map/pallas_call | solution.py:270
  25.1 0.6 %copy.8 = f32[4,512]{1,0:T(4,128)} copy(f32[4,512]{1,0:T(4,128)S(1)} %shard_map.64) | data formatting | bytes 16384
Async XLA Ops:
  0.0 1.5 %copy-start = (bf16[1,512,1920]{2,1,0:T(8,128)(2,1)S(1)}, bf16[1,512,1920]{2,1,0:T(8,128)(2,1)}, u32[]{:S(2)}) copy-start(bf16[1,512,1920]{2,1,0:T(8,128)(2,1)} %q_hbm.1) | copy-start | bytes 5898244
  1.5 0.9 %copy-start.1 = (bf16[4,16,1536]{2,1,0:T(8,128)(2,1)S(1)}, bf16[4,16,1536]{2,1,0:T(8,128)(2,1)}, u32[]{:S(2)}) copy-start(bf16[4,16,1536]{2,1,0:T(8,128)(2,1)} %in_ref.1) | copy-start | bytes 589828
  2.5 0.9 %copy-start.2 = (bf16[4,16,1280]{2,1,0:T(8,128)(2,1)S(1)}, bf16[4,16,1280]{2,1,0:T(8,128)(2,1)}, u32[]{:S(2)}) copy-start(bf16[4,16,1280]{2,1,0:T(8,128)(2,1)} %out_ref.1) | copy-start | bytes 491524
  3.4 0.7 %copy-start.3 = (s32[16]{0:T(128)S(1)}, s32[16]{0:T(128)}, u32[]{:S(2)}) copy-start(s32[16]{0:T(128)} %owner_ref.1) | copy-start | bytes 196
  4.0 0.7 %copy-start.4 = (s32[4]{0:T(128)S(1)}, s32[4]{0:T(128)}, u32[]{:S(2)}) copy-start(s32[4]{0:T(128)} %len_ref.1) | copy-start | bytes 52

commit v2 on v1

v2 whole, which is shorter than its diff:
```python
import functools
import math

import jax
import jax.numpy as jnp
from jax import lax
from jax.experimental import pallas as pl
from jax.experimental.pallas import tpu as pltpu
from jax.sharding import PartitionSpec as P

MESH = pl.DeviceIdType.MESH
F32 = jnp.float32
BF16 = jnp.bfloat16
NT = (((1,), (1,)), ((), ()))

LANES = 128
WIDE = 256
PACK = 16
SUB = 8
BLOCK = LANES // PACK


def nt(a, b):
    return lax.dot_general(a, b, NT, preferred_element_type=F32)


def over(a, k):
    return lax.shift_right_logical(a, k.bit_length() - 1) if k & (k - 1) == 0 else a // k


def mod(a, k):
    return lax.bitwise_and(a, k - 1) if k & (k - 1) == 0 else lax.rem(a, k)


def iota(shape, dim):
    return lax.broadcasted_iota(jnp.int32, shape, dim)


def kernel(
    n,
    owner_hbm,
    len_hbm,
    in_hbm,
    out_hbm,
    f_hbm,
    q_hbm,
    res_ref,
    owner_ref,
    len_ref,
    in_ref,
    out_ref,
    f_v,
    q_v,
    it_ref,
    ot_ref,
    gt_ref,
    p_ref,
    send_ref,
    recv_ref,
    rs_send,
    rs_recv,
    mine_ref,
    f_sem,
    small_sem,
    g_send_sem,
    g_recv_sem,
    s_send_sem,
    s_recv_sem,
):
    me = lax.axis_index("mod")
    rows = in_ref.shape[0]
    grad = f_hbm.shape[1]
    queries = q_hbm.shape[1]
    seq = math.isqrt(in_ref.shape[2] * out_ref.shape[2] // grad)
    rank_in = in_ref.shape[2] // seq
    rank_out = out_ref.shape[2] // seq
    quarters = PACK // rows
    outer = rank_out // quarters
    depth = outer * rank_in
    blocks = n // BLOCK
    chunks_in = in_ref.shape[2] // WIDE
    chunks_out = out_ref.shape[2] // WIDE
    in_low = WIDE // seq
    out_low = WIDE // (seq * quarters)
    f_blocks = f_sem.shape[0]
    f_rows = grad // f_blocks
    span = rows * n

    def f_copy(b):
        where = pl.ds(b * f_rows, f_rows)
        return pltpu.make_async_copy(f_hbm.at[0, where], f_v.at[where], f_sem.at[b])

    small = [
        pltpu.make_async_copy(src, dst, small_sem.at[i])
        for i, (src, dst) in enumerate(
            (
                (owner_hbm, owner_ref),
                (len_hbm, len_ref),
                (in_hbm, in_ref),
                (out_hbm, out_ref),
                (q_hbm.at[0], q_v),
            )
        )
    ]
    for copy in small:
        copy.start()
    for b in range(f_blocks):
        f_copy(b).start()

    barrier = pltpu.get_barrier_semaphore()

    @pl.loop(1, n)
    def _(k):
        pl.semaphore_signal(
            barrier, inc=1, device_id={"mod": lax.rem(me + k, n)}, device_id_type=MESH
        )

    a = iota((WIDE, WIDE), 0)
    b = iota((WIDE, WIDE), 1)
    swap = ((over(a, in_low) == mod(b, seq)) & (mod(a, in_low) == over(b, seq))).astype(BF16)
    a = iota((out_low * seq, WIDE), 0)
    b = iota((out_low * seq, WIDE), 1)
    fold = ((over(a, seq) == over(b, seq * quarters)) & (mod(a, seq) == mod(b, seq))).astype(BF16)
    eye = (iota((LANES, LANES), 0) == iota((LANES, LANES), 1)).astype(BF16)

    gt_ref[pl.ds(depth, gt_ref.shape[0] - depth), :] = jnp.zeros(
        (gt_ref.shape[0] - depth, LANES), F32
    )
    for s in range(quarters):
        p_ref[s, pl.ds(depth, p_ref.shape[1] - depth), :] = jnp.zeros(
            (p_ref.shape[1] - depth, queries), BF16
        )

    for copy in small[:2]:
        copy.wait()

    lane = mod(iota((1, span), 1), n)
    held = jnp.zeros((1, span), jnp.int32)
    if n <= 32:
        for m in range(n):
            held = jnp.where(lane == m, owner_ref[m], held)
    else:
        held = lax.fori_loop(
            0, n, lambda m, v: jnp.where(lane == m, owner_ref[m], v), held
        )

    a = iota((LANES, WIDE), 0)
    b = iota((LANES, WIDE), 1)
    limit = jnp.zeros((LANES, WIDE), jnp.int32)
    for e in range(rows):
        limit = jnp.where(mod(a, rows) == e, len_ref[e], limit)
    live = (mod(b, seq) < limit) & (mod(over(b, seq), quarters) == over(mod(a, PACK), rows))

    for copy in small[2:4]:
        copy.wait()

    def block_at(p):
        return lax.rem(over(me, BLOCK) + 1 + p, blocks)

    def peer(p, s):
        return block_at(p) * BLOCK + mod(me + s, BLOCK)

    def g_copy(dst, slot):
        return pltpu.make_async_remote_copy(
            src_ref=send_ref.at[dst],
            dst_ref=recv_ref.at[slot],
            send_sem=g_send_sem.at[dst],
            recv_sem=g_recv_sem.at[slot],
            device_id={"mod": dst},
            device_id_type=MESH,
        )

    def s_copy(dst, slot):
        return pltpu.make_async_remote_copy(
            src_ref=rs_send.at[dst],
            dst_ref=rs_recv.at[slot],
            send_sem=s_send_sem.at[dst],
            recv_sem=s_recv_sem.at[slot],
            device_id={"mod": dst},
            device_id_type=MESH,
        )

    @pl.loop(0, blocks)
    def _(p):
        row = iota((LANES, span), 0)
        col = iota((LANES, span), 1)
        pick = (
            (held == block_at(p) * BLOCK + over(row, PACK)) & (over(col, n) == mod(row, rows))
        ).astype(BF16)

        for c in range(chunks_out):
            x = out_ref[:, :, c * WIDE : (c + 1) * WIDE].reshape(span, WIDE)
            y = jnp.dot(pick, x, preferred_element_type=F32)
            y = jnp.where(live, y, 0.0).astype(BF16)
            ot_ref[pl.ds(c * out_low * seq, out_low * seq), :] = nt(fold, y)
        for c in range(chunks_in):
            x = in_ref[:, :, c * WIDE : (c + 1) * WIDE].reshape(span, WIDE)
            y = jnp.dot(pick, x, preferred_element_type=F32).astype(BF16)
            it_ref[c] = nt(swap, y)

        step = outer // 2
        for first in range(0, outer, step):

            def add(t8, acc):
                acc = list(acc)
                base = pl.multiple_of(t8 * SUB, SUB)
                fos = [ot_ref[pl.ds((first + o) * seq + base, SUB), :] for o in range(step)]
                for tt in range(SUB):
                    t = t8 * SUB + tt
                    fi = [
                        it_ref[c, pl.ds(pl.multiple_of(t * in_low, in_low), in_low), :]
                        for c in range(chunks_in)
                    ]
                    for o in range(step):
                        fo = fos[o][tt : tt + 1]
                        for c in range(chunks_in):
                            acc[o * chunks_in + c] = acc[o * chunks_in + c] + fi[c] * fo
                return tuple(acc)

            acc = lax.fori_loop(
                0,
                seq // SUB,
                add,
                tuple(jnp.zeros((in_low, LANES), F32) for _ in range(step * chunks_in)),
            )
            for o in range(step):
                for c in range(chunks_in):
                    gt_ref[pl.ds((first + o) * rank_in + c * in_low, in_low), :] = acc[
                        o * chunks_in + c
                    ]

        formed = nt(eye, gt_ref[...].astype(BF16)).astype(BF16)
        send_ref[pl.ds(block_at(p) * BLOCK, BLOCK)] = formed.reshape(
            BLOCK, PACK, formed.shape[1]
        )

        @pl.when(p == 0)
        def _():
            pl.semaphore_wait(barrier, n - 1)

        @pl.loop(0, BLOCK)
        def _(s):
            dst = peer(p, s)

            @pl.when(dst != me)
            def _():
                g_copy(dst, me).start()

    recv_ref[me] = send_ref[me]

    small[4].wait()
    for blk in range(f_blocks):
        f_copy(blk).wait()
        part = nt(f_v[blk * f_rows : (blk + 1) * f_rows, :], q_v[...]).astype(BF16)
        for o in range(f_rows // rank_in):
            whole = blk * (f_rows // rank_in) + o
            p_ref[whole % quarters, pl.ds((whole // quarters) * rank_in, rank_in), :] = part[
                o * rank_in : (o + 1) * rank_in
            ]

    @pl.loop(0, blocks)
    def _(back):
        p = blocks - 1 - back

        @pl.loop(0, BLOCK)
        def _(s):
            src = peer(p, s)

            @pl.when(src != me)
            def _():
                g_copy(src, src).wait_recv()

        got = recv_ref[pl.ds(block_at(p) * BLOCK, BLOCK)].reshape(LANES, p_ref.shape[1])
        row = iota(got.shape, 0)
        total = jnp.zeros((LANES, queries), F32)
        for s in range(quarters):
            mine = (over(mod(row, PACK), rows) == s).astype(F32).astype(BF16)
            total = total + jnp.dot(got * mine, p_ref[s], preferred_element_type=F32)
        total = total.reshape(BLOCK, PACK, queries)
        total = total[:, :SUB] + total[:, SUB:]
        total = total + pltpu.roll(total, rows, 1)
        width = queries // quarters
        low = iota((BLOCK, SUB, width), 1) < rows
        pieces = [
            jnp.where(
                low,
                total[:, :, 2 * i * width : (2 * i + 1) * width],
                total[:, :, (2 * i + 1) * width : (2 * i + 2) * width],
            )
            for i in range(quarters // 2)
        ]
        total = jnp.concatenate(pieces, axis=1)
        mine_ref[pl.ds(block_at(p) * BLOCK, BLOCK)] = total
        rs_send[pl.ds(block_at(p) * BLOCK, BLOCK)] = total.astype(BF16)

        @pl.loop(0, BLOCK)
        def _(s):
            dst = peer(p, s)

            @pl.when(dst != me)
            def _():
                s_copy(dst, me).start()

    rs_recv[me] = jnp.zeros(rs_recv.shape[1:], BF16)

    @pl.loop(1, n)
    def _(k):
        src = lax.rem(me + n - k, n)
        s_copy(src, src).wait_recv()

    total = mine_ref[me]
    if n <= 32:
        for src in range(n):
            total = total + rs_recv[src].astype(F32)
    else:
        total = lax.fori_loop(0, n, lambda src, v: v + rs_recv[src].astype(F32), total)
    width = queries // quarters
    for s in range(quarters):
        res_ref[:, s * width : (s + 1) * width] = total[s * rows : (s + 1) * rows]

    @pl.loop(1, n)
    def _(k):
        dst = lax.rem(me + k, n)
        g_copy(dst, me).wait_send()
        s_copy(dst, me).wait_send()


def local(n, inputs_proj, outputs_proj, lengths, owner, fisher_inv, query_grads):
    rows = inputs_proj.shape[0]
    grad = fisher_inv.shape[1]
    queries = query_grads.shape[1]
    quarters = PACK // rows
    depth = grad // quarters
    padded = -(-depth // LANES) * LANES
    f_blocks = 4
    return pl.pallas_call(
        functools.partial(kernel, n),
        out_shape=jax.ShapeDtypeStruct((rows, queries), F32),
        in_specs=[pl.BlockSpec(memory_space=pltpu.HBM)] * 6,
        out_specs=pl.BlockSpec(memory_space=pltpu.VMEM),
        scratch_shapes=[
            pltpu.SMEM(owner.shape, jnp.int32),
            pltpu.SMEM(lengths.shape, jnp.int32),
            pltpu.VMEM(inputs_proj.shape, BF16),
            pltpu.VMEM(outputs_proj.shape, BF16),
            pltpu.VMEM((grad, grad), BF16),
            pltpu.VMEM((queries, grad), BF16),
            pltpu.VMEM((inputs_proj.shape[2] // WIDE, WIDE, LANES), F32),
            pltpu.VMEM((outputs_proj.shape[2] // quarters, LANES), F32),
            pltpu.VMEM((padded, LANES), F32),
            pltpu.VMEM((quarters, padded, queries), BF16),
            pltpu.VMEM((n, PACK, padded), BF16),
            pltpu.VMEM((n, PACK, padded), BF16),
            pltpu.VMEM((n, PACK, queries // quarters), BF16),
            pltpu.VMEM((n, PACK, queries // quarters), BF16),
            pltpu.VMEM((n, PACK, queries // quarters), F32),
            pltpu.SemaphoreType.DMA((f_blocks,)),
            pltpu.SemaphoreType.DMA((5,)),
            pltpu.SemaphoreType.DMA((n,)),
            pltpu.SemaphoreType.DMA((n,)),
            pltpu.SemaphoreType.DMA((n,)),
            pltpu.SemaphoreType.DMA((n,)),
        ],
        compiler_params=pltpu.CompilerParams(
            collective_id=0, has_side_effects=True, vmem_limit_bytes=64 * 1024 * 1024
        ),
    )(owner, lengths, inputs_proj, outputs_proj, fisher_inv, query_grads)


def solution(mesh):
    return jax.shard_map(
        functools.partial(local, mesh.shape["mod"]),
        mesh=mesh,
        in_specs=(
            P(("grp", "mod"), None, None),
            P(("grp", "mod"), None, None),
            P(("grp", "mod")),
            P(),
            P("mod", None, None),
            P("mod", None, None),
        ),
        out_specs=P(("grp", "mod"), None),
        check_vma=False,
    )
```

time: 26 us -> 22.9 us (0.88)
  local copies, waits for them, and re-layouts: 5.3 us -> 1.3 us
  Pallas kernels: 20.4 us -> 21.4 us
    unnamed x11 -> x1, local copies, waits for them, and re-layouts: 5.3 us -> 1.3 us
    pallas_call x1, Pallas kernels: 20.4 us -> 21.4 us  [local(): pl.pallas_call(functools.partial(kernel, n), out_shape=jax.ShapeDtypeStru...]
where the time goes in v2:
time: 22.9 us; the launch traced here: 22.7 us
  Pallas kernels  21.4 us (93%)
  local copies, waits for them, and re-layouts  1.3 us (6%)
    pallas_call x1, Pallas kernels, local(): pl.pallas_call(functools.partial(kernel, n), out_shape=jax.ShapeDtypeStru...  21.4 us
    unnamed x1, local copies, waits for them, and re-layouts  1.3 us

profile of v2, /device:TPU:0, one launch (start us, length us, event | category | flops | bytes accessed | tf_op | source)
XLA Modules:
  0.0 22.7 jit_solution(10919916856917036850)
XLA Ops:
  0.0 21.4 %shard_map.64 = f32[4,512]{1,0:T(4,128)} custom-call(s32[16]{0:T(128)} %owner_hbm.1, s32[4]{0:T(128)} %len_hbm.1, bf16[4,16,1536]{2,1,0:T(8,128)(2,1)} %in_hbm.1, bf16[4,16,1280]{2,1,0:T(8,128)(2,1)} %out_hbm.1, bf16[1,1920,1920]{2,1,0:T(8,128)(2,1)} %f_hbm.1, bf16[1,512,1920]{2,1,0:T(8,128)(2,1)} %q_hbm.1), custom_call_target="tpu_custom_call" | custom-call | tf_op jit(solution)/shard_map/pallas_call | solution.py:336
  21.4 1.3 %copy.8 = f32[4,512]{1,0:T(4,128)} copy(f32[4,512]{1,0:T(4,128)} %shard_map.64) | data formatting | bytes 16384

commit v3 on v2

--- a/solution.py
+++ b/solution.py
@@ -30,6 +30,14 @@
 
 def mod(a, k):
     return lax.bitwise_and(a, k - 1) if k & (k - 1) == 0 else lax.rem(a, k)
+
+
+def each(low, high, body, most=16):
+    if high - low <= most:
+        for k in range(low, high):
+            body(k)
+    else:
+        pl.loop(low, high)(body)
 
 
 def iota(shape, dim):
@@ -109,11 +117,12 @@
 
     barrier = pltpu.get_barrier_semaphore()
 
-    @pl.loop(1, n)
-    def _(k):
+    def greet(k):
         pl.semaphore_signal(
-            barrier, inc=1, device_id={"mod": lax.rem(me + k, n)}, device_id_type=MESH
-        )
+            barrier, inc=1, device_id={"mod": mod(me + k, n)}, device_id_type=MESH
+        )
+
+    each(1, n, greet)
 
     a = iota((WIDE, WIDE), 0)
     b = iota((WIDE, WIDE), 1)
@@ -155,33 +164,36 @@
         copy.wait()
 
     def block_at(p):
-        return lax.rem(over(me, BLOCK) + 1 + p, blocks)
+        return mod(over(me, BLOCK) + 1 + p, blocks)
 
     def peer(p, s):
         return block_at(p) * BLOCK + mod(me + s, BLOCK)
 
-    def g_copy(dst, slot):
+    def g_copy(dst):
         return pltpu.make_async_remote_copy(
             src_ref=send_ref.at[dst],
-            dst_ref=recv_ref.at[slot],
-            send_sem=g_send_sem.at[dst],
-            recv_sem=g_recv_sem.at[slot],
+            dst_ref=recv_ref.at[me],
+            send_sem=g_send_sem,
+            recv_sem=g_recv_sem.at[over(me, BLOCK)],
             device_id={"mod": dst},
             device_id_type=MESH,
         )
 
-    def s_copy(dst, slot):
+    def s_copy(dst):
         return pltpu.make_async_remote_copy(
             src_ref=rs_send.at[dst],
-            dst_ref=rs_recv.at[slot],
-            send_sem=s_send_sem.at[dst],
-            recv_sem=s_recv_sem.at[slot],
+            dst_ref=rs_recv.at[me],
+            send_sem=s_send_sem,
+            recv_sem=s_recv_sem,
             device_id={"mod": dst},
             device_id_type=MESH,
         )
 
-    @pl.loop(0, blocks)
-    def _(p):
+    def wait_for(ref, count, sem):
+        part = ref.at[pl.ds(0, count)]
+        pltpu.make_async_copy(part, part, sem).wait()
+
+    def form(p, own):
         row = iota((LANES, span), 0)
         col = iota((LANES, span), 1)
         pick = (
@@ -201,28 +213,13 @@
         step = outer // 2
         for first in range(0, outer, step):
 
-            def add(t8, acc):
-                acc = list(acc)
-                base = pl.multiple_of(t8 * SUB, SUB)
-                fos = [ot_ref[pl.ds((first + o) * seq + base, SUB), :] for o in range(step)]
-                for tt in range(SUB):
-                    t = t8 * SUB + tt
-                    fi = [
-                        it_ref[c, pl.ds(pl.multiple_of(t * in_low, in_low), in_low), :]
-                        for c in range(chunks_in)
-                    ]
-                    for o in range(step):
-                        fo = fos[o][tt : tt + 1]
-                        for c in range(chunks_in):
-                            acc[o * chunks_in + c] = acc[o * chunks_in + c] + fi[c] * fo
-                return tuple(acc)
-
-            acc = lax.fori_loop(
-                0,
-                seq // SUB,
-                add,
-                tuple(jnp.zeros((in_low, LANES), F32) for _ in range(step * chunks_in)),
-            )
+            acc = [jnp.zeros((in_low, LANES), F32)] * (step * chunks_in)
+            for t in range(seq):
+                fi = [it_ref[c, t * in_low : (t + 1) * in_low, :] for c in range(chunks_in)]
+                for o in range(step):
+                    fo = ot_ref[(first + o) * seq + t : (first + o) * seq + t + 1, :]
+                    for c in range(chunks_in):
+                        acc[o * chunks_in + c] = acc[o * chunks_in + c] + fi[c] * fo
             for o in range(step):
                 for c in range(chunks_in):
                     gt_ref[pl.ds((first + o) * rank_in + c * in_low, in_low), :] = acc[
@@ -234,18 +231,14 @@
             BLOCK, PACK, formed.shape[1]
         )
 
-        @pl.when(p == 0)
-        def _():
-            pl.semaphore_wait(barrier, n - 1)
-
-        @pl.loop(0, BLOCK)
-        def _(s):
-            dst = peer(p, s)
-
-            @pl.when(dst != me)
-            def _():
-                g_copy(dst, me).start()
-
+        if own:
+            each(1, BLOCK, lambda s: g_copy(peer(p, s)).start())
+        else:
+            each(0, BLOCK, lambda s: g_copy(peer(p, s)).start())
+
+    pl.semaphore_wait(barrier, n - 1)
+    each(0, blocks - 1, lambda p: form(p, False), 2)
+    form(blocks - 1, True)
     recv_ref[me] = send_ref[me]
 
     small[4].wait()
@@ -258,18 +251,8 @@
                 o * rank_in : (o + 1) * rank_in
             ]
 
-    @pl.loop(0, blocks)
-    def _(back):
-        p = blocks - 1 - back
-
-        @pl.loop(0, BLOCK)
-        def _(s):
-            src = peer(p, s)
-
-            @pl.when(src != me)
-            def _():
-                g_copy(src, src).wait_recv()
-
+    def score(p, own):
+        wait_for(recv_ref, BLOCK - 1 if own else BLOCK, g_recv_sem.at[block_at(p)])
         got = recv_ref[pl.ds(block_at(p) * BLOCK, BLOCK)].reshape(LANES, p_ref.shape[1])
         row = iota(got.shape, 0)
         total = jnp.zeros((LANES, queries), F32)
@@ -293,20 +276,15 @@
         mine_ref[pl.ds(block_at(p) * BLOCK, BLOCK)] = total
         rs_send[pl.ds(block_at(p) * BLOCK, BLOCK)] = total.astype(BF16)
 
-        @pl.loop(0, BLOCK)
-        def _(s):
-            dst = peer(p, s)
-
-            @pl.when(dst != me)
-            def _():
-                s_copy(dst, me).start()
-
+        if own:
+            each(1, BLOCK, lambda s: s_copy(peer(p, s)).start())
+        else:
+            each(0, BLOCK, lambda s: s_copy(peer(p, s)).start())
+
+    score(blocks - 1, True)
+    each(0, blocks - 1, lambda p: score(p, False), 2)
     rs_recv[me] = jnp.zeros(rs_recv.shape[1:], BF16)
-
-    @pl.loop(1, n)
-    def _(k):
-        src = lax.rem(me + n - k, n)
-        s_copy(src, src).wait_recv()
+    wait_for(rs_recv, n - 1, s_recv_sem)
 
     total = mine_ref[me]
     if n <= 32:
@@ -318,11 +296,8 @@
     for s in range(quarters):
         res_ref[:, s * width : (s + 1) * width] = total[s * rows : (s + 1) * rows]
 
-    @pl.loop(1, n)
-    def _(k):
-        dst = lax.rem(me + k, n)
-        g_copy(dst, me).wait_send()
-        s_copy(dst, me).wait_send()
+    wait_for(send_ref, n - 1, g_send_sem)
+    wait_for(rs_send, n - 1, s_send_sem)
 
 
 def local(n, inputs_proj, outputs_proj, lengths, owner, fisher_inv, query_grads):
@@ -356,10 +331,10 @@
             pltpu.VMEM((n, PACK, queries // quarters), F32),
             pltpu.SemaphoreType.DMA((f_blocks,)),
             pltpu.SemaphoreType.DMA((5,)),
-            pltpu.SemaphoreType.DMA((n,)),
-            pltpu.SemaphoreType.DMA((n,)),
-            pltpu.SemaphoreType.DMA((n,)),
-            pltpu.SemaphoreType.DMA((n,)),
+            pltpu.SemaphoreType.DMA,
+            pltpu.SemaphoreType.DMA((n // BLOCK,)),
+            pltpu.SemaphoreType.DMA,
+            pltpu.SemaphoreType.DMA,
         ],
         compiler_params=pltpu.CompilerParams(
             collective_id=0, has_side_effects=True, vmem_limit_bytes=64 * 1024 * 1024

time: 22.9 us -> 21.6 us (0.943)
  Pallas kernels: 21.4 us -> 20.1 us
    pallas_call x1, Pallas kernels: 21.4 us -> 20.1 us  [local(): pl.pallas_call(functools.partial(kernel, n), out_shape=jax.ShapeDtypeStru...]
where the time goes in v3:
time: 21.6 us; the launch traced here: 21.4 us
  Pallas kernels  20.1 us (93%)
  local copies, waits for them, and re-layouts  1.3 us (6%)
    pallas_call x1, Pallas kernels, local(): pl.pallas_call(functools.partial(kernel, n), out_shape=jax.ShapeDtypeStru...  20.1 us
    unnamed x1, local copies, waits for them, and re-layouts  1.3 us

profile of v3, /device:TPU:0, one launch (start us, length us, event | category | flops | bytes accessed | tf_op | source)
XLA Modules:
  0.0 21.4 jit_solution(10061062054641710124)
XLA Ops:
  0.0 20.1 %shard_map.64 = f32[4,512]{1,0:T(4,128)} custom-call(s32[16]{0:T(128)} %owner_hbm.1, s32[4]{0:T(128)} %len_hbm.1, bf16[4,16,1536]{2,1,0:T(8,128)(2,1)} %in_hbm.1, bf16[4,16,1280]{2,1,0:T(8,128)(2,1)} %out_hbm.1, bf16[1,1920,1920]{2,1,0:T(8,128)(2,1)} %f_hbm.1, bf16[1,512,1920]{2,1,0:T(8,128)(2,1)} %q_hbm.1), custom_call_target="tpu_custom_call" | custom-call | tf_op jit(solution)/shard_map/pallas_call | solution.py:311
  20.1 1.3 %copy.8 = f32[4,512]{1,0:T(4,128)} copy(f32[4,512]{1,0:T(4,128)} %shard_map.64) | data formatting | bytes 16384

commit v4 on v3

--- a/solution.py
+++ b/solution.py
@@ -18,6 +18,7 @@
 PACK = 16
 SUB = 8
 BLOCK = LANES // PACK
+PLANE = BLOCK // 2
 
 
 def nt(a, b):
@@ -166,15 +167,31 @@
     def block_at(p):
         return mod(over(me, BLOCK) + 1 + p, blocks)
 
-    def peer(p, s):
-        return block_at(p) * BLOCK + mod(me + s, BLOCK)
+    def plane_at(p, h):
+        return block_at(p) * 2 + mod(over(me, PLANE) + h, 2)
+
+    def peer(p, h, s):
+        return plane_at(p, h) * PLANE + mod(me + s, PLANE)
+
+    def peers(p, own):
+        return [
+            peer(p, h, s) for h in range(2) for s in range(1 if own and h == 0 else 0, PLANE)
+        ]
+
+    def precondition(blk):
+        part = nt(f_v[blk * f_rows : (blk + 1) * f_rows, :], q_v[...]).astype(BF16)
+        for o in range(f_rows // rank_in):
+            whole = blk * (f_rows // rank_in) + o
+            p_ref[whole % quarters, pl.ds((whole // quarters) * rank_in, rank_in), :] = part[
+                o * rank_in : (o + 1) * rank_in
+            ]
 
     def g_copy(dst):
         return pltpu.make_async_remote_copy(
             src_ref=send_ref.at[dst],
             dst_ref=recv_ref.at[me],
             send_sem=g_send_sem,
-            recv_sem=g_recv_sem.at[over(me, BLOCK)],
+            recv_sem=g_recv_sem.at[over(me, PLANE)],
             device_id={"mod": dst},
             device_id_type=MESH,
         )
@@ -194,6 +211,10 @@
         pltpu.make_async_copy(part, part, sem).wait()
 
     def form(p, own):
+        if own:
+            small[4].wait()
+            for blk in range(early):
+                f_copy(blk).wait()
         row = iota((LANES, span), 0)
         col = iota((LANES, span), 1)
         pick = (
@@ -212,7 +233,8 @@
 
         step = outer // 2
         for first in range(0, outer, step):
-
+            if own:
+                precondition(first // step)
             acc = [jnp.zeros((in_low, LANES), F32)] * (step * chunks_in)
             for t in range(seq):
                 fi = [it_ref[c, t * in_low : (t + 1) * in_low, :] for c in range(chunks_in)]
@@ -231,39 +253,41 @@
             BLOCK, PACK, formed.shape[1]
         )
 
-        if own:
-            each(1, BLOCK, lambda s: g_copy(peer(p, s)).start())
+        if isinstance(p, int):
+            if p == 0:
+                pl.semaphore_wait(barrier, n - 1)
         else:
-            each(0, BLOCK, lambda s: g_copy(peer(p, s)).start())
-
-    pl.semaphore_wait(barrier, n - 1)
+            pl.when(p == 0)(lambda: pl.semaphore_wait(barrier, n - 1))
+        for dst in peers(p, own):
+            g_copy(dst).start()
+
+    early = 2
     each(0, blocks - 1, lambda p: form(p, False), 2)
     form(blocks - 1, True)
     recv_ref[me] = send_ref[me]
 
-    small[4].wait()
-    for blk in range(f_blocks):
+    for blk in range(early, f_blocks):
         f_copy(blk).wait()
-        part = nt(f_v[blk * f_rows : (blk + 1) * f_rows, :], q_v[...]).astype(BF16)
-        for o in range(f_rows // rank_in):
-            whole = blk * (f_rows // rank_in) + o
-            p_ref[whole % quarters, pl.ds((whole // quarters) * rank_in, rank_in), :] = part[
-                o * rank_in : (o + 1) * rank_in
-            ]
-
-    def score(p, own):
-        wait_for(recv_ref, BLOCK - 1 if own else BLOCK, g_recv_sem.at[block_at(p)])
-        got = recv_ref[pl.ds(block_at(p) * BLOCK, BLOCK)].reshape(LANES, p_ref.shape[1])
+        precondition(blk)
+
+    def score(p, own, halves):
+        count = len(halves) * PLANE
+        for h in halves:
+            wait_for(
+                recv_ref, PLANE - 1 if own and h == 0 else PLANE, g_recv_sem.at[plane_at(p, h)]
+            )
+        start = block_at(p) * BLOCK if len(halves) == 2 else plane_at(p, halves[0]) * PLANE
+        got = recv_ref[pl.ds(start, count)].reshape(count * PACK, p_ref.shape[1])
         row = iota(got.shape, 0)
-        total = jnp.zeros((LANES, queries), F32)
+        total = jnp.zeros((count * PACK, queries), F32)
         for s in range(quarters):
             mine = (over(mod(row, PACK), rows) == s).astype(F32).astype(BF16)
             total = total + jnp.dot(got * mine, p_ref[s], preferred_element_type=F32)
-        total = total.reshape(BLOCK, PACK, queries)
+        total = total.reshape(count, PACK, queries)
         total = total[:, :SUB] + total[:, SUB:]
         total = total + pltpu.roll(total, rows, 1)
         width = queries // quarters
-        low = iota((BLOCK, SUB, width), 1) < rows
+        low = iota((count, SUB, width), 1) < rows
         pieces = [
             jnp.where(
                 low,
@@ -273,16 +297,19 @@
             for i in range(quarters // 2)
         ]
         total = jnp.concatenate(pieces, axis=1)
-        mine_ref[pl.ds(block_at(p) * BLOCK, BLOCK)] = total
-        rs_send[pl.ds(block_at(p) * BLOCK, BLOCK)] = total.astype(BF16)
-
-        if own:
-            each(1, BLOCK, lambda s: s_copy(peer(p, s)).start())
-        else:
-            each(0, BLOCK, lambda s: s_copy(peer(p, s)).start())
-
-    score(blocks - 1, True)
-    each(0, blocks - 1, lambda p: score(p, False), 2)
+        mine_ref[pl.ds(start, count)] = total
+        rs_send[pl.ds(start, count)] = total.astype(BF16)
+
+        for h in halves:
+            for s in range(1 if own and h == 0 else 0, PLANE):
+                s_copy(peer(p, h, s)).start()
+
+    def score_block(p):
+        score(p, False, [0])
+        score(p, False, [1])
+
+    score(blocks - 1, True, [0, 1])
+    each(0, blocks - 1, score_block, 2)
     rs_recv[me] = jnp.zeros(rs_recv.shape[1:], BF16)
     wait_for(rs_recv, n - 1, s_recv_sem)
 
@@ -332,7 +359,7 @@
             pltpu.SemaphoreType.DMA((f_blocks,)),
             pltpu.SemaphoreType.DMA((5,)),
             pltpu.SemaphoreType.DMA,
-            pltpu.SemaphoreType.DMA((n // BLOCK,)),
+            pltpu.SemaphoreType.DMA((n // PLANE,)),
             pltpu.SemaphoreType.DMA,
             pltpu.SemaphoreType.DMA,
         ],

time: 21.6 us -> 21.7 us (level)
  no operation moved by 1% of the time
where the time goes in v4:
time: 21.7 us; the launch traced here: 21.4 us
  Pallas kernels  20.1 us (93%)
  local copies, waits for them, and re-layouts  1.3 us (6%)
    pallas_call x1, Pallas kernels, local(): pl.pallas_call(functools.partial(kernel, n), out_shape=jax.ShapeDtypeStru...  20.1 us
    unnamed x1, local copies, waits for them, and re-layouts  1.3 us

profile of v4, /device:TPU:0, one launch (start us, length us, event | category | flops | bytes accessed | tf_op | source)
XLA Modules:
  0.0 21.4 jit_solution(15980002373946688177)
XLA Ops:
  0.0 20.1 %shard_map.64 = f32[4,512]{1,0:T(4,128)} custom-call(s32[16]{0:T(128)} %owner_hbm.1, s32[4]{0:T(128)} %len_hbm.1, bf16[4,16,1536]{2,1,0:T(8,128)(2,1)} %in_hbm.1, bf16[4,16,1280]{2,1,0:T(8,128)(2,1)} %out_hbm.1, bf16[1,1920,1920]{2,1,0:T(8,128)(2,1)} %f_hbm.1, bf16[1,512,1920]{2,1,0:T(8,128)(2,1)} %q_hbm.1), custom_call_target="tpu_custom_call" | custom-call | tf_op jit(solution)/shard_map/pallas_call | solution.py:338
  20.1 1.3 %copy.8 = f32[4,512]{1,0:T(4,128)} copy(f32[4,512]{1,0:T(4,128)} %shard_map.64) | data formatting | bytes 16384

commit v5 on v3

--- a/solution.py
+++ b/solution.py
@@ -231,12 +231,16 @@
             BLOCK, PACK, formed.shape[1]
         )
 
+        if isinstance(p, int):
+            if p == 0:
+                pl.semaphore_wait(barrier, n - 1)
+        else:
+            pl.when(p == 0)(lambda: pl.semaphore_wait(barrier, n - 1))
         if own:
             each(1, BLOCK, lambda s: g_copy(peer(p, s)).start())
         else:
             each(0, BLOCK, lambda s: g_copy(peer(p, s)).start())
 
-    pl.semaphore_wait(barrier, n - 1)
     each(0, blocks - 1, lambda p: form(p, False), 2)
     form(blocks - 1, True)
     recv_ref[me] = send_ref[me]
@@ -307,7 +311,7 @@
     quarters = PACK // rows
     depth = grad // quarters
     padded = -(-depth // LANES) * LANES
-    f_blocks = 4
+    f_blocks = 1
     return pl.pallas_call(
         functools.partial(kernel, n),
         out_shape=jax.ShapeDtypeStruct((rows, queries), F32),

time: 21.6 us -> 20.2 us (0.935)
  Pallas kernels: 20.1 us -> 18.7 us
    pallas_call x1, Pallas kernels: 20.1 us -> 18.7 us  [local(): pl.pallas_call(functools.partial(kernel, n), out_shape=jax.ShapeDtypeStru...]
where the time goes in v5:
time: 20.2 us; the launch traced here: 20 us
  Pallas kernels  18.7 us (93%)
  local copies, waits for them, and re-layouts  1.3 us (6%)
    pallas_call x1, Pallas kernels, local(): pl.pallas_call(functools.partial(kernel, n), out_shape=jax.ShapeDtypeStru...  18.7 us
    unnamed x1, local copies, waits for them, and re-layouts  1.3 us

profile of v5, /device:TPU:0, one launch (start us, length us, event | category | flops | bytes accessed | tf_op | source)
XLA Modules:
  0.0 20.0 jit_solution(2244591284500846233)
XLA Ops:
  0.0 18.7 %shard_map.64 = f32[4,512]{1,0:T(4,128)} custom-call(s32[16]{0:T(128)} %owner_hbm.1, s32[4]{0:T(128)} %len_hbm.1, bf16[4,16,1536]{2,1,0:T(8,128)(2,1)} %in_hbm.1, bf16[4,16,1280]{2,1,0:T(8,128)(2,1)} %out_hbm.1, bf16[1,1920,1920]{2,1,0:T(8,128)(2,1)} %f_hbm.1, bf16[1,512,1920]{2,1,0:T(8,128)(2,1)} %q_hbm.1), custom_call_target="tpu_custom_call" | custom-call | tf_op jit(solution)/shard_map/pallas_call | solution.py:315
  18.7 1.3 %copy.8 = f32[4,512]{1,0:T(4,128)} copy(f32[4,512]{1,0:T(4,128)} %shard_map.64) | data formatting | bytes 16384

commit v6 on v5

--- a/solution.py
+++ b/solution.py
@@ -193,7 +193,18 @@
         part = ref.at[pl.ds(0, count)]
         pltpu.make_async_copy(part, part, sem).wait()
 
+    def precondition(half):
+        cols = pl.ds(half * (queries // 2), queries // 2)
+        part = nt(f_v[...], q_v[cols, :]).astype(BF16)
+        for o in range(rank_out):
+            p_ref[o % quarters, pl.ds((o // quarters) * rank_in, rank_in), cols] = part[
+                o * rank_in : (o + 1) * rank_in
+            ]
+
     def form(p, own):
+        if own:
+            small[4].wait()
+            f_copy(0).wait()
         row = iota((LANES, span), 0)
         col = iota((LANES, span), 1)
         pick = (
@@ -211,6 +222,8 @@
             it_ref[c] = nt(swap, y)
 
         step = outer // 2
+        if own:
+            precondition(0)
         for first in range(0, outer, step):
 
             acc = [jnp.zeros((in_low, LANES), F32)] * (step * chunks_in)
@@ -245,15 +258,7 @@
     form(blocks - 1, True)
     recv_ref[me] = send_ref[me]
 
-    small[4].wait()
-    for blk in range(f_blocks):
-        f_copy(blk).wait()
-        part = nt(f_v[blk * f_rows : (blk + 1) * f_rows, :], q_v[...]).astype(BF16)
-        for o in range(f_rows // rank_in):
-            whole = blk * (f_rows // rank_in) + o
-            p_ref[whole % quarters, pl.ds((whole // quarters) * rank_in, rank_in), :] = part[
-                o * rank_in : (o + 1) * rank_in
-            ]
+    precondition(1)
 
     def score(p, own):
         wait_for(recv_ref, BLOCK - 1 if own else BLOCK, g_recv_sem.at[block_at(p)])

time: 20.2 us -> 21.2 us (1.050)
  Pallas kernels: 18.7 us -> 19.7 us
    pallas_call x1, Pallas kernels: 18.7 us -> 19.7 us  [local(): pl.pallas_call(functools.partial(kernel, n), out_shape=jax.ShapeDtypeStru...]
where the time goes in v6:
time: 21.2 us; the launch traced here: 21 us
  Pallas kernels  19.7 us (93%)
  local copies, waits for them, and re-layouts  1.3 us (6%)
    pallas_call x1, Pallas kernels, local(): pl.pallas_call(functools.partial(kernel, n), out_shape=jax.ShapeDtypeStru...  19.7 us
    unnamed x1, local copies, waits for them, and re-layouts  1.3 us

profile of v6, /device:TPU:0, one launch (start us, length us, event | category | flops | bytes accessed | tf_op | source)
XLA Modules:
  0.0 21.0 jit_solution(11951542571207950248)
XLA Ops:
  0.0 19.7 %shard_map.64 = f32[4,512]{1,0:T(4,128)} custom-call(s32[16]{0:T(128)} %owner_hbm.1, s32[4]{0:T(128)} %len_hbm.1, bf16[4,16,1536]{2,1,0:T(8,128)(2,1)} %in_hbm.1, bf16[4,16,1280]{2,1,0:T(8,128)(2,1)} %out_hbm.1, bf16[1,1920,1920]{2,1,0:T(8,128)(2,1)} %f_hbm.1, bf16[1,512,1920]{2,1,0:T(8,128)(2,1)} %q_hbm.1), custom_call_target="tpu_custom_call" | custom-call | tf_op jit(solution)/shard_map/pallas_call | solution.py:320
  19.7 1.3 %copy.8 = f32[4,512]{1,0:T(4,128)} copy(f32[4,512]{1,0:T(4,128)} %shard_map.64) | data formatting | bytes 16384

commit v7 on v5

--- a/solution.py
+++ b/solution.py
@@ -106,10 +106,15 @@
                 (len_hbm, len_ref),
                 (in_hbm, in_ref),
                 (out_hbm, out_ref),
-                (q_hbm.at[0], q_v),
             )
         )
     ]
+    q_rows = queries // 4
+    for i in range(4):
+        where = pl.ds(i * q_rows, q_rows)
+        small.append(
+            pltpu.make_async_copy(q_hbm.at[0, where], q_v.at[where], small_sem.at[4 + i])
+        )
     for copy in small:
         copy.start()
     for b in range(f_blocks):
@@ -245,15 +250,15 @@
     form(blocks - 1, True)
     recv_ref[me] = send_ref[me]
 
-    small[4].wait()
+    for copy in small[4:]:
+        copy.wait()
     for blk in range(f_blocks):
         f_copy(blk).wait()
-        part = nt(f_v[blk * f_rows : (blk + 1) * f_rows, :], q_v[...]).astype(BF16)
-        for o in range(f_rows // rank_in):
-            whole = blk * (f_rows // rank_in) + o
-            p_ref[whole % quarters, pl.ds((whole // quarters) * rank_in, rank_in), :] = part[
-                o * rank_in : (o + 1) * rank_in
-            ]
+    part = nt(f_v[...], q_v[...]).astype(BF16)
+    for o in range(rank_out):
+        p_ref[o % quarters, pl.ds((o // quarters) * rank_in, rank_in), :] = part[
+            o * rank_in : (o + 1) * rank_in
+        ]
 
     def score(p, own):
         wait_for(recv_ref, BLOCK - 1 if own else BLOCK, g_recv_sem.at[block_at(p)])
@@ -311,7 +316,7 @@
     quarters = PACK // rows
     depth = grad // quarters
     padded = -(-depth // LANES) * LANES
-    f_blocks = 1
+    f_blocks = 8
     return pl.pallas_call(
         functools.partial(kernel, n),
         out_shape=jax.ShapeDtypeStruct((rows, queries), F32),
@@ -334,7 +339,7 @@
             pltpu.VMEM((n, PACK, queries // quarters), BF16),
             pltpu.VMEM((n, PACK, queries // quarters), F32),
             pltpu.SemaphoreType.DMA((f_blocks,)),
-            pltpu.SemaphoreType.DMA((5,)),
+            pltpu.SemaphoreType.DMA((4 + 4,)),
             pltpu.SemaphoreType.DMA,
             pltpu.SemaphoreType.DMA((n // BLOCK,)),
             pltpu.SemaphoreType.DMA,

time: 20.2 us -> 20.5 us (1.015)
  Pallas kernels: 18.7 us -> 19 us
    pallas_call x1, Pallas kernels: 18.7 us -> 19 us  [local(): pl.pallas_call(functools.partial(kernel, n), out_shape=jax.ShapeDtypeStru...]
where the time goes in v7:
time: 20.5 us; the launch traced here: 20.3 us
  Pallas kernels  19 us (93%)
  local copies, waits for them, and re-layouts  1.3 us (6%)
    pallas_call x1, Pallas kernels, local(): pl.pallas_call(functools.partial(kernel, n), out_shape=jax.ShapeDtypeStru...  19 us
    unnamed x1, local copies, waits for them, and re-layouts  1.3 us

profile of v7, /device:TPU:0, one launch (start us, length us, event | category | flops | bytes accessed | tf_op | source)
XLA Modules:
  0.0 20.3 jit_solution(3178777145353050403)
XLA Ops:
  0.0 19.0 %shard_map.64 = f32[4,512]{1,0:T(4,128)} custom-call(s32[16]{0:T(128)} %owner_hbm.1, s32[4]{0:T(128)} %len_hbm.1, bf16[4,16,1536]{2,1,0:T(8,128)(2,1)} %in_hbm.1, bf16[4,16,1280]{2,1,0:T(8,128)(2,1)} %out_hbm.1, bf16[1,1920,1920]{2,1,0:T(8,128)(2,1)} %f_hbm.1, bf16[1,512,1920]{2,1,0:T(8,128)(2,1)} %q_hbm.1), custom_call_target="tpu_custom_call" | custom-call | tf_op jit(solution)/shard_map/pallas_call | solution.py:320
  19.0 1.3 %copy.8 = f32[4,512]{1,0:T(4,128)} copy(f32[4,512]{1,0:T(4,128)} %shard_map.64) | data formatting | bytes 16384
